TPU v7x, 32 devices: a whole 2x2x4 slice. The times are simulated.
32 devices in a mesh: tm: 4 (over y, core), rows: 8 (over z, x).
Axes of the slice: x: 2, y: 2, z: 4, core: 2. Of those that a mesh axis runs over, the one named last changes fastest.
Arguments:
- features: bfloat16 [16, 16, 320, 128], P('tm', 'rows'), may hold values from -20 to 20
- gain_one: float32 [128], replicated, may hold values from 0.1 to 1.9
- shift_one: float32 [128], replicated, may hold values from -4 to 4
- weight_one: bfloat16 [3456, 128], replicated, may hold values from -0.109375 to 0.109375
- bias_one: float32 [128], replicated, may hold values from -6 to 6
- gain_two: float32 [128], replicated, may hold values from 0.1 to 1.9
- shift_two: float32 [128], replicated, may hold values from -4 to 4
- weight_two: bfloat16 [3456, 128], replicated, may hold values from -0.109375 to 0.109375
- bias_two: float32 [128], replicated, may hold values from -6 to 6
Outputs:
- block_out: bfloat16 [16, 16, 320, 128], P('tm', 'rows')
All inputs are finite; a program needn't handle non-finite values.
Results may differ from a plain program's by a relative error of at most 0.007.
Values may be sent and summed in bfloat16 or wider, within the bound.
A program may use at most 64 MiB of HBM per device.

v0:
```python
import jax
import jax.numpy as jnp
from jax import lax
from jax.sharding import PartitionSpec as P

C = 128
GROUPS = 32


EPS = 1e-06


def extended_2(cells, sides, width):
    for axis, dim in sides:
        count = lax.axis_size(axis)
        ends = count - 1
        head = lax.slice_in_dim(cells, 0, width, axis=dim)
        tail = lax.slice_in_dim(cells, cells.shape[dim] - width, cells.shape[dim], axis=dim)
        cells = jnp.concatenate(
            [
                lax.ppermute(tail, axis, [(i, (i + 1) % count) for i in range(ends)]),
                cells,
                lax.ppermute(head, axis, [((i + 1) % count, i) for i in range(ends)]),
            ],
            axis=dim,
        )
    return cells


def shifted(block, axis, distance):
    devices = range(lax.axis_size(axis))
    route = [(i - distance, i) for i in devices if i - distance in devices]
    return lax.ppermute(block, axis, route)


def group_sums(values):
    per_channel = jnp.sum(values, axis=(0, 1, 2))
    return jnp.sum(per_channel.reshape(GROUPS, -1), axis=1)


def moments(values, cell_count):
    first_sum, square_sum = lax.psum(
        (group_sums(values), group_sums(values * values)), ("tm", "rows")
    )
    average = first_sum / cell_count
    spread = square_sum / cell_count - average * average
    return (average, spread)


def activate(values, average, spread, gain, shift):
    center = jnp.repeat(average, C // GROUPS)
    factor = jnp.repeat(lax.rsqrt(spread + EPS), C // GROUPS)
    normed = (values - center) * factor * gain + shift
    return jax.nn.silu(normed).astype(jnp.bfloat16)


def border(values, depth, width):
    padded = extended_2(values, (("rows", 1),), width)
    carried = shifted(padded[padded.shape[0] - depth :], "tm", 1)
    return jnp.concatenate([carried, padded], 0)


def repeat_first(extended, depth):
    first_span = lax.axis_index("tm") == 0
    leading = jnp.broadcast_to(extended[depth : depth + 1], extended[:depth].shape)
    replaced = jnp.concatenate([leading, extended[depth:]], 0)
    return jnp.where(first_span, replaced, extended)


def valid_conv(padded, weight, bias):
    out_frames = padded.shape[0] - 2
    out_rows = padded.shape[1] - 2
    width_cells = padded.shape[2]
    channels = padded.shape[3]
    widened = jnp.pad(padded, ((0, 0), (0, 0), (1, 1), (0, 0)))
    summed = jnp.zeros((out_frames, out_rows, width_cells, channels), jnp.float32)
    for time_tap in range(3):
        for row_tap in range(3):
            columns = jnp.concatenate(
                [
                    widened[
                        time_tap : time_tap + out_frames,
                        row_tap : row_tap + out_rows,
                        col_tap : col_tap + width_cells,
                    ]
                    for col_tap in range(3)
                ],
                -1,
            )
            first_row = (time_tap * 3 + row_tap) * 3 * channels
            taps_block = weight[first_row : first_row + 3 * channels]
            summed = summed + jnp.einsum(
                "frwk,kc->frwc", columns, taps_block, preferred_element_type=jnp.float32
            )
    return summed + bias


def body(
    features, gain_one, shift_one, weight_one, bias_one, gain_two, shift_two, weight_two, bias_two
):
    inputs = features.astype(jnp.float32)
    frames_dev, rows_dev, width_cells = (features.shape[0], features.shape[1], features.shape[2])
    cell_count = (
        frames_dev
        * rows_dev
        * width_cells
        * (C // GROUPS)
        * lax.axis_size("tm")
        * lax.axis_size("rows")
    )
    average, spread = moments(inputs, cell_count)
    activated = activate(inputs, average, spread, gain_one, shift_one)
    hidden = valid_conv(repeat_first(border(activated, 2, 1), 2), weight_one, bias_one).astype(
        jnp.bfloat16
    )
    hidden_wide = hidden.astype(jnp.float32)
    average_two, spread_two = moments(hidden_wide, cell_count)
    second = activate(hidden_wide, average_two, spread_two, gain_two, shift_two)
    second = repeat_first(border(second, 2, 1), 2)
    result = valid_conv(second, weight_two, bias_two) + inputs
    return result.astype(jnp.bfloat16)


def solution(mesh):
    in_specs = (P("tm", "rows", None, None), P(), P(), P(), P(), P(), P(), P(), P())
    out_specs = P("tm", "rows", None, None)
    return jax.shard_map(body, mesh=mesh, in_specs=in_specs, out_specs=out_specs, check_vma=False)
```

profile of v0, /device:TPU:12, one launch (start us, length us, event | category | flops | bytes accessed | tf_op | source)
XLA Modules:
  0.0 170.4 jit_solution(10641356617571351171)
XLA Ops:
  0.0 1.4 convert_reduce_fusion
  1.4 0.1 reshape.22
  1.5 0.1 reshape.23
  1.7 0.1 reduce_sum.73
  1.8 0.1 reduce_sum.75
  1.9 41.2 %all-reduce.3 = (f32[32]{0:T(128)S(1)}, f32[32]{0:T(128)S(1)}) all-reduce(f32[32]{0:T(128)S(1)} %reduce_sum.75, f32[32]{0:T(128)S(1)} %reduce_sum.73), channel_id=1, replica_groups=mesh['tm'=4,'rows'=8] {'tm','rows'}, use_global_device_ids=true, to_apply=%region_5.0 | all-reduce | flops 64 | bytes 512 | tf_op jit(solution)/shard_map/psum | solution.py:42
  43.1 0.1 broadcast_in_dim.32
  43.2 0.1 sub.26
  43.3 0.1 broadcast_in_dim.33
  43.4 0.1 mul.57
  43.5 1.6 fusion.188
  45.1 2.5 %collective-permute-start = (bf16[4,1,320,128]{3,2,1,0:T(8,128)(2,1)S(1)}, bf16[4,1,320,128]{3,2,1,0:T(8,128)(2,1)S(1)}, u32[]{:S(2)}, u32[]{:S(2)}) collective-permute-start(bf16[4,1,320,128]{3,2,1,0:T(8,128)(2,1)S(1)} %get-tuple-element.69), channel_id=1, source_target_pairs={{0,1},{1,2},{2,3},{3,4},{4,5},{5,6},{6,7},{8,9},{9,10},{10,11},{11... | collective-permute-start | bytes 983048 | tf_op jit(solution)/shard_map/ppermute | solution.py:21
  47.6 4.3 %collective-permute-start.1 = (bf16[4,1,320,128]{3,2,1,0:T(8,128)(2,1)S(1)}, bf16[4,1,320,128]{3,2,1,0:T(8,128)(2,1)S(1)}, u32[]{:S(2)}, u32[]{:S(2)}) collective-permute-start(bf16[4,1,320,128]{3,2,1,0:T(8,128)(2,1)S(1)} %get-tuple-element.70), channel_id=1, source_target_pairs={{1,0},{2,1},{3,2},{4,3},{5,4},{6,5},{7,6},{9,8},{10,9},{11,10},{12... | collective-permute-start | bytes 983048 | tf_op jit(solution)/shard_map/ppermute | solution.py:23
  51.9 8.9 %collective-permute-done = bf16[4,1,320,128]{3,2,1,0:T(8,128)(2,1)S(1)} collective-permute-done((bf16[4,1,320,128]{3,2,1,0:T(8,128)(2,1)S(1)}, bf16[4,1,320,128]{3,2,1,0:T(8,128)(2,1)S(1)}, u32[]{:S(2)}, u32[]{:S(2)}) %collective-permute-start) | collective-permute-done | bytes 327712 | tf_op jit(solution)/shard_map/ppermute | solution.py:21
  60.8 1.9 %collective-permute-done.1 = bf16[4,1,320,128]{3,2,1,0:T(8,128)(2,1)S(1)} collective-permute-done((bf16[4,1,320,128]{3,2,1,0:T(8,128)(2,1)S(1)}, bf16[4,1,320,128]{3,2,1,0:T(8,128)(2,1)S(1)}, u32[]{:S(2)}, u32[]{:S(2)}) %collective-permute-start.1) | collective-permute-done | bytes 327712 | tf_op jit(solution)/shard_map/ppermute | solution.py:23
  62.7 0.1 pad_maximum_fusion.4
  62.8 1.9 %collective-permute-start.2 = (bf16[2,4,320,128]{3,2,1,0:T(8,128)(2,1)S(1)}, bf16[2,4,320,128]{3,2,1,0:T(8,128)(2,1)S(1)}, u32[]{:S(2)}, u32[]{:S(2)}) collective-permute-start(bf16[2,4,320,128]{3,2,1,0:T(8,128)(2,1)S(1)} %pad_maximum_fusion.4), channel_id=1, source_target_pairs={{0,8},{8,16},{16,24},{1,9},{9,17},{17,25},{2,10},{10,18},{18,26},{... | collective-permute-start | bytes 1966088 | tf_op jit(solution)/shard_map/ppermute | solution.py:33
  64.7 9.9 %collective-permute-done.2 = bf16[2,4,320,128]{3,2,1,0:T(8,128)(2,1)S(1)} collective-permute-done((bf16[2,4,320,128]{3,2,1,0:T(8,128)(2,1)S(1)}, bf16[2,4,320,128]{3,2,1,0:T(8,128)(2,1)S(1)}, u32[]{:S(2)}, u32[]{:S(2)}) %collective-permute-start.2) | collective-permute-done | bytes 655392 | tf_op jit(solution)/shard_map/ppermute | solution.py:33
  74.7 0.1 broadcast_in_dim.35
  74.8 0.3 maximum_select_fusion
  75.0 1.0 fusion.247
  76.0 2.1 %fusion.246 = (bf16[4,2,320,128]{3,2,1,0:T(8,128)(2,1)S(1)}, bf16[4,2,320,128]{3,2,1,0:T(8,128)(2,1)S(1)}, bf16[4,2,320,128]{3,2,1,0:T(8,128)(2,1)S(1)}, bf16[4,...) fusion(bf16[6,4,320,128]{3,2,1,0:T(8,128)(2,1)S(1)} %maximum_se, ...), kind=kLoop, calls=%fused_computation.261 | loop fusion | bytes 9175040 | tf_op jit(solution)/shard_map/slice | solution.py:81
  78.1 1.9 %pad_slice_fusion.35 = (bf16[4,2,320,128]{3,2,1,0:T(8,128)(2,1)S(1)}, bf16[4,2,320,128]{3,2,1,0:T(8,128)(2,1)S(1)}, bf16[4,2,320,128]{3,2,1,0:T(8,128)(2,1)S(1)}...) fusion(bf16[6,4,320,128]{3,2,1,0:T(8,128)(2,1)S(1)} %maximum_se, ...), kind=kLoop, calls=%fused_computation.258 | loop fusion | bytes 9175040 | tf_op jit(solution)/shard_map/slice | solution.py:81
  80.0 0.7 fusion.30
  80.7 0.7 fusion.36
  81.4 0.7 fusion.42
  82.1 0.7 fusion.48
  82.8 0.7 fusion.24
  83.4 0.7 fusion.6
  84.1 0.7 fusion.12
  84.8 0.7 fusion.18
  85.5 1.1 convert_reduce_fusion.1
  86.6 0.1 reshape.24
  86.7 0.1 reduce_sum.77
  86.8 0.1 reshape.25
  86.9 0.1 reduce_sum.79
  87.1 39.2 %all-reduce.2 = (f32[32]{0:T(128)S(1)}, f32[32]{0:T(128)S(1)}) all-reduce(f32[32]{0:T(128)S(1)} %reduce_sum.79, f32[32]{0:T(128)S(1)} %reduce_sum.77), channel_id=1, replica_groups=mesh['tm'=4,'rows'=8] {'tm','rows'}, use_global_device_ids=true, to_apply=%region_11.12 | all-reduce | flops 64 | bytes 512 | tf_op jit(solution)/shard_map/psum | solution.py:42
  126.2 0.1 broadcast_in_dim.36
  126.3 0.1 sub.30
  126.4 0.1 broadcast_in_dim.37
  126.5 0.1 mul.65
  126.6 0.5 fusion.178
  127.2 3.4 %collective-permute-start.3 = (bf16[4,1,320,128]{3,2,1,0:T(8,128)(2,1)S(1)}, bf16[4,1,320,128]{3,2,1,0:T(8,128)(2,1)S(1)}, u32[]{:S(2)}, u32[]{:S(2)}) collective-permute-start(bf16[4,1,320,128]{3,2,1,0:T(8,128)(2,1)S(1)} %get-tuple-element.67), channel_id=1, source_target_pairs={{0,1},{1,2},{2,3},{3,4},{4,5},{5,6},{6,7},{8,9},{9,10},{10,11},{11... | collective-permute-start | bytes 983048 | tf_op jit(solution)/shard_map/ppermute | solution.py:21
  130.6 3.5 %collective-permute-start.4 = (bf16[4,1,320,128]{3,2,1,0:T(8,128)(2,1)S(1)}, bf16[4,1,320,128]{3,2,1,0:T(8,128)(2,1)S(1)}, u32[]{:S(2)}, u32[]{:S(2)}) collective-permute-start(bf16[4,1,320,128]{3,2,1,0:T(8,128)(2,1)S(1)} %get-tuple-element.68), channel_id=1, source_target_pairs={{1,0},{2,1},{3,2},{4,3},{5,4},{6,5},{7,6},{9,8},{10,9},{11,10},{12... | collective-permute-start | bytes 983048 | tf_op jit(solution)/shard_map/ppermute | solution.py:23
  134.1 8.7 %collective-permute-done.3 = bf16[4,1,320,128]{3,2,1,0:T(8,128)(2,1)S(1)} collective-permute-done((bf16[4,1,320,128]{3,2,1,0:T(8,128)(2,1)S(1)}, bf16[4,1,320,128]{3,2,1,0:T(8,128)(2,1)S(1)}, u32[]{:S(2)}, u32[]{:S(2)}) %collective-permute-start.3) | collective-permute-done | bytes 327712 | tf_op jit(solution)/shard_map/ppermute | solution.py:21
  142.8 2.6 %collective-permute-done.4 = bf16[4,1,320,128]{3,2,1,0:T(8,128)(2,1)S(1)} collective-permute-done((bf16[4,1,320,128]{3,2,1,0:T(8,128)(2,1)S(1)}, bf16[4,1,320,128]{3,2,1,0:T(8,128)(2,1)S(1)}, u32[]{:S(2)}, u32[]{:S(2)}) %collective-permute-start.4) | collective-permute-done | bytes 327712 | tf_op jit(solution)/shard_map/ppermute | solution.py:23
  145.5 0.1 pad_maximum_fusion.2
  145.5 1.9 %collective-permute-start.5 = (bf16[2,4,320,128]{3,2,1,0:T(8,128)(2,1)S(1)}, bf16[2,4,320,128]{3,2,1,0:T(8,128)(2,1)S(1)}, u32[]{:S(2)}, u32[]{:S(2)}) collective-permute-start(bf16[2,4,320,128]{3,2,1,0:T(8,128)(2,1)S(1)} %pad_maximum_fusion.2), channel_id=1, source_target_pairs={{0,8},{8,16},{16,24},{1,9},{9,17},{17,25},{2,10},{10,18},{18,26},{... | collective-permute-start | bytes 1966088 | tf_op jit(solution)/shard_map/ppermute | solution.py:33
  147.5 9.9 %collective-permute-done.5 = bf16[2,4,320,128]{3,2,1,0:T(8,128)(2,1)S(1)} collective-permute-done((bf16[2,4,320,128]{3,2,1,0:T(8,128)(2,1)S(1)}, bf16[2,4,320,128]{3,2,1,0:T(8,128)(2,1)S(1)}, u32[]{:S(2)}, u32[]{:S(2)}) %collective-permute-start.5) | collective-permute-done | bytes 655392 | tf_op jit(solution)/shard_map/ppermute | solution.py:33
  157.4 0.1 broadcast_in_dim.39
  157.5 0.3 maximum_select_fusion.1
  157.8 1.0 fusion.245
  158.8 2.0 %fusion.244 = (bf16[4,2,320,128]{3,2,1,0:T(8,128)(2,1)S(1)}, bf16[4,2,320,128]{3,2,1,0:T(8,128)(2,1)S(1)}, bf16[4,2,320,128]{3,2,1,0:T(8,128)(2,1)S(1)}, bf16[4,...) fusion(bf16[6,4,320,128]{3,2,1,0:T(8,128)(2,1)S(1)} %maximum_se, ...), kind=kLoop, calls=%fused_computation.259 | loop fusion | bytes 9175040 | tf_op jit(solution)/shard_map/slice | solution.py:81
  160.8 1.9 %pad_slice_fusion.17 = (bf16[4,2,320,128]{3,2,1,0:T(8,128)(2,1)S(1)}, bf16[4,2,320,128]{3,2,1,0:T(8,128)(2,1)S(1)}, bf16[4,2,320,128]{3,2,1,0:T(8,128)(2,1)S(1)}...) fusion(bf16[6,4,320,128]{3,2,1,0:T(8,128)(2,1)S(1)} %maximum_se, ...), kind=kLoop, calls=%fused_computation.240 | loop fusion | bytes 9175040 | tf_op jit(solution)/shard_map/slice | solution.py:81
  162.7 0.7 fusion.84
  163.4 0.7 fusion.90
  164.1 0.7 fusion.96
  164.8 0.7 fusion.102
  165.4 0.7 fusion.78
  166.1 0.7 fusion.60
  166.8 0.7 fusion.66
  167.5 0.7 fusion.72
  168.2 0.4 copy-done
  168.6 1.8 %fusion.164 = bf16[4,2,320,128]{3,2,1,0:T(8,128)(2,1)} fusion(bf16[4,2,320,128]{3,2,1,0:T(8,128)(2,1)S(1)} %copy-done, f32[4,2,320,128]{3,2,1,0:T(8,128)S(1)} %fusion.102, f32[4,2,320,128]{3,2,1,0:T(8,128)S(1)} %fusion.96, f32[4,2,320,128]{3,2,1,0:T(8,128)S(1)} %fusion.90, f32[4,2,320,128]{3,2,1,0:T(8,128)S(1)} %fusion.84, ...), kind=kOutput, calls=%fused_computation.137 | convolution fusion | flops 261488640 | bytes 13861376 | tf_op jit(solution)/shard_map/frwk,kc->frwc/dot_general | solution.py:92
  (19 shorter events, 0.2 us)
Async XLA Ops:
  45.1 15.6 %collective-permute-start = (bf16[4,1,320,128]{3,2,1,0:T(8,128)(2,1)S(1)}, bf16[4,1,320,128]{3,2,1,0:T(8,128)(2,1)S(1)}, u32[]{:S(2)}, u32[]{:S(2)}) collective-permute-start(bf16[4,1,320,128]{3,2,1,0:T(8,128)(2,1)S(1)} %get-tuple-element.69), channel_id=1, source_target_pairs={{0,1},{1,2},{2,3},{3,4},{4,5},{5,6},{6,7},{8,9},{9,10},{10,11},{11... | collective-permute-start | bytes 983048 | tf_op jit(solution)/shard_map/ppermute | solution.py:21
  47.6 15.1 %collective-permute-start.1 = (bf16[4,1,320,128]{3,2,1,0:T(8,128)(2,1)S(1)}, bf16[4,1,320,128]{3,2,1,0:T(8,128)(2,1)S(1)}, u32[]{:S(2)}, u32[]{:S(2)}) collective-permute-start(bf16[4,1,320,128]{3,2,1,0:T(8,128)(2,1)S(1)} %get-tuple-element.70), channel_id=1, source_target_pairs={{1,0},{2,1},{3,2},{4,3},{5,4},{6,5},{7,6},{9,8},{10,9},{11,10},{12... | collective-permute-start | bytes 983048 | tf_op jit(solution)/shard_map/ppermute | solution.py:23
  62.8 11.9 %collective-permute-start.2 = (bf16[2,4,320,128]{3,2,1,0:T(8,128)(2,1)S(1)}, bf16[2,4,320,128]{3,2,1,0:T(8,128)(2,1)S(1)}, u32[]{:S(2)}, u32[]{:S(2)}) collective-permute-start(bf16[2,4,320,128]{3,2,1,0:T(8,128)(2,1)S(1)} %pad_maximum_fusion.4), channel_id=1, source_target_pairs={{0,8},{8,16},{16,24},{1,9},{9,17},{17,25},{2,10},{10,18},{18,26},{... | collective-permute-start | bytes 1966088 | tf_op jit(solution)/shard_map/ppermute | solution.py:33
  78.1 1.9 %copy-start.1 = (bf16[3456,128]{1,0:T(8,128)(2,1)S(1)}, bf16[3456,128]{1,0:T(8,128)(2,1)}, u32[]{:S(2)}) copy-start(bf16[3456,128]{1,0:T(8,128)(2,1)} %param.12) | copy-start | bytes 2654212
  84.8 0.7 copy-start.3
  85.5 41.1 %copy-start.5 = (f32[128]{0:T(128)S(1)}, f32[128]{0:T(128)}, u32[]{:S(2)}) copy-start(f32[128]{0:T(128)} %param.15) | copy-start | bytes 1540
  85.5 41.1 %copy-start.6 = (f32[128]{0:T(128)S(1)}, f32[128]{0:T(128)}, u32[]{:S(2)}) copy-start(f32[128]{0:T(128)} %param.14) | copy-start | bytes 1540
  127.2 15.6 %collective-permute-start.3 = (bf16[4,1,320,128]{3,2,1,0:T(8,128)(2,1)S(1)}, bf16[4,1,320,128]{3,2,1,0:T(8,128)(2,1)S(1)}, u32[]{:S(2)}, u32[]{:S(2)}) collective-permute-start(bf16[4,1,320,128]{3,2,1,0:T(8,128)(2,1)S(1)} %get-tuple-element.67), channel_id=1, source_target_pairs={{0,1},{1,2},{2,3},{3,4},{4,5},{5,6},{6,7},{8,9},{9,10},{10,11},{11... | collective-permute-start | bytes 983048 | tf_op jit(solution)/shard_map/ppermute | solution.py:21
  130.6 14.9 %collective-permute-start.4 = (bf16[4,1,320,128]{3,2,1,0:T(8,128)(2,1)S(1)}, bf16[4,1,320,128]{3,2,1,0:T(8,128)(2,1)S(1)}, u32[]{:S(2)}, u32[]{:S(2)}) collective-permute-start(bf16[4,1,320,128]{3,2,1,0:T(8,128)(2,1)S(1)} %get-tuple-element.68), channel_id=1, source_target_pairs={{1,0},{2,1},{3,2},{4,3},{5,4},{6,5},{7,6},{9,8},{10,9},{11,10},{12... | collective-permute-start | bytes 983048 | tf_op jit(solution)/shard_map/ppermute | solution.py:23
  145.5 11.9 %collective-permute-start.5 = (bf16[2,4,320,128]{3,2,1,0:T(8,128)(2,1)S(1)}, bf16[2,4,320,128]{3,2,1,0:T(8,128)(2,1)S(1)}, u32[]{:S(2)}, u32[]{:S(2)}) collective-permute-start(bf16[2,4,320,128]{3,2,1,0:T(8,128)(2,1)S(1)} %pad_maximum_fusion.2), channel_id=1, source_target_pairs={{0,8},{8,16},{16,24},{1,9},{9,17},{17,25},{2,10},{10,18},{18,26},{... | collective-permute-start | bytes 1966088 | tf_op jit(solution)/shard_map/ppermute | solution.py:33
  160.8 1.9 %copy-start.2 = (bf16[3456,128]{1,0:T(8,128)(2,1)S(1)}, bf16[3456,128]{1,0:T(8,128)(2,1)}, u32[]{:S(2)}) copy-start(bf16[3456,128]{1,0:T(8,128)(2,1)} %param.16) | copy-start | bytes 2654212
  167.5 1.1 copy-start
  167.5 1.1 copy-start.4
where the time goes:
time: 171 us; the launch traced here: 170 us
  blocking collectives  80.4 us (47%)
  waiting for transfers between devices  42 us (25%)
  starting transfers between devices  17.5 us (10%)
  matrix products  13.6 us (8%)
  local copies, waits for them, and re-layouts  11.6 us (7%)
  other arithmetic  4.76 us (3%)
    psum x2, blocking collectives, moments(): lax.psum((group_sums(values), group_sums(values * values)), ('tm', 'rows'))  80.4 us
    ppermute x2, waiting for transfers between devices, shifted(): return lax.ppermute(block, axis, route)  19.8 us
    ppermute x2, waiting for transfers between devices, extended_2(): lax.ppermute(tail, axis, [(i, (i + 1) % count) for i in range(ends)])  17.6 us
    dot_general x18, matrix products, valid_conv(): jnp.einsum('frwk,kc->frwc', columns, taps_block, preferred_element_type=j...  13.6 us
    slice x6, local copies, waits for them, and re-layouts, valid_conv(): widened[time_tap:time_tap + out_frames, row_tap:row_tap + out_rows, col_t...  9.84 us
    ppermute x2, starting transfers between devices, extended_2(): lax.ppermute(head, axis, [((i + 1) % count, i) for i in range(ends)])  7.81 us
    ppermute x2, starting transfers between devices, extended_2(): lax.ppermute(tail, axis, [(i, (i + 1) % count) for i in range(ends)])  5.85 us
    ppermute x2, waiting for transfers between devices, extended_2(): lax.ppermute(head, axis, [((i + 1) % count, i) for i in range(ends)])  4.53 us
  transfers between devices with their start and end apart: 6, of which 6 were waited for; matrix products, arithmetic and copies ran while one was open for 0% of the time, Pallas kernels for 0%

commit v1 on v0

v1 whole, which is shorter than its diff:
```python
import functools

import jax
import jax.numpy as jnp
from jax import lax
from jax.experimental import pallas as pl
from jax.experimental.pallas import tpu as pltpu
from jax.sharding import PartitionSpec as P

GROUPS = 32
EPS = 1e-06
LEAD = 2
STAT_ROWS = 8


def group_total(values, size):
    lanes = values.shape[-1]
    lane = lax.broadcasted_iota(jnp.int32, values.shape, 1)
    step = 1
    while step < size:
        left = pltpu.roll(values, step, 1)
        right = pltpu.roll(values, lanes - step, 1)
        values = values + jnp.where((lane & step) == 0, right, left)
        step *= 2
    return values


def kernel(
    tm_count, row_count,
    x_ref, gain1_ref, shift1_ref, w1_ref, bias1_ref, gain2_ref, shift2_ref, w2_ref, bias2_ref,
    out_ref,
    act, big1, big2, hid, up, dn, pre, mine, stat_a, stat_b,
    w_sem, send_sem, recv_sem, sa_send, sa_recv, sb_send, sb_recv,
):
    frames, rows, width, chans = x_ref.shape
    tm = lax.axis_index("tm")
    row = lax.axis_index("rows")
    has_up = row > 0
    has_dn = row < row_count - 1
    has_prev = tm > 0
    has_next = tm < tm_count - 1
    span = 3 * chans
    depth = 3 * span
    size = chans // GROUPS
    total = float(frames * rows * width * size * tm_count * row_count)

    def weight_copies(which, src, dst):
        return [
            pltpu.make_async_copy(
                src.at[pl.ds(i * depth, depth)],
                dst.at[i, pl.ds(o * span, depth), pl.ds(o * chans, chans)],
                w_sem.at[which, i * rows + o],
            )
            for i in range(3)
            for o in range(rows)
        ]

    loads1 = weight_copies(0, w1_ref, big1)
    loads2 = weight_copies(1, w2_ref, big2)
    for copy in loads1 + loads2:
        copy.start()

    barrier = pltpu.get_barrier_semaphore()
    for k in range(1, row_count):
        pl.semaphore_signal(barrier, inc=1, device_id={"rows": lax.rem(row + k, row_count)})
    for k in range(1, tm_count):
        pl.semaphore_signal(barrier, inc=1, device_id={"tm": lax.rem(tm + k, tm_count)})
    pl.semaphore_wait(barrier, row_count + tm_count - 2)

    def halo(phase, src):
        early, late = frames - LEAD, LEAD
        below = {"rows": jnp.minimum(row + 1, row_count - 1)}
        above = {"rows": jnp.maximum(row - 1, 0)}
        after = {"tm": jnp.minimum(tm + 1, tm_count - 1)}

        def copy(n, source, target, device):
            return pltpu.make_async_remote_copy(
                src_ref=source, dst_ref=target,
                send_sem=send_sem.at[phase, n], recv_sem=recv_sem.at[phase, n],
                device_id=device,
            )

        u, d, p = up.at[phase], dn.at[phase], pre.at[phase]
        return {
            "down_late": copy(0, src.at[pl.ds(early, late), rows - 1], u.at[pl.ds(LEAD + early, late)], below),
            "up_late": copy(1, src.at[pl.ds(early, late), 0], d.at[pl.ds(LEAD + early, late)], above),
            "down_early": copy(2, src.at[pl.ds(0, early), rows - 1], u.at[pl.ds(LEAD, early)], below),
            "up_early": copy(3, src.at[pl.ds(0, early), 0], d.at[pl.ds(LEAD, early)], above),
            "next": copy(4, src.at[pl.ds(early, late)], p, after),
            "corner_up": copy(5, u.at[pl.ds(LEAD + early, late)], u.at[pl.ds(0, LEAD)], after),
            "corner_dn": copy(6, d.at[pl.ds(LEAD + early, late)], d.at[pl.ds(0, LEAD)], after),
        }

    def when(cond, fn):
        pl.when(cond)(fn)

    def send_late(c):
        when(has_dn, c["down_late"].start)
        when(has_up, c["up_late"].start)
        when(has_next, c["next"].start)

    def send_early(c):
        when(has_dn, c["down_early"].start)
        when(has_up, c["up_early"].start)

    def forward(c):
        @pl.when(has_up)
        def _():
            c["down_late"].wait_recv()
            when(has_next, c["corner_up"].start)

        @pl.when(has_dn)
        def _():
            c["up_late"].wait_recv()
            when(has_next, c["corner_dn"].start)

    def finish_sends(c):
        @pl.when(has_dn)
        def _():
            c["down_late"].wait_send()
            c["down_early"].wait_send()
            when(has_next, c["corner_dn"].wait_send)

        @pl.when(has_up)
        def _():
            c["up_late"].wait_send()
            c["up_early"].wait_send()
            when(has_next, c["corner_up"].wait_send)

        when(has_next, c["next"].wait_send)

    def reduce_stats(phase, src):
        first = jnp.zeros((8, chans), jnp.float32)
        square = jnp.zeros((8, chans), jnp.float32)

        def add(n, carry):
            s, q = carry
            v = src[n // rows, n % rows].astype(jnp.float32).reshape(width // 8, 8, chans)
            return s + jnp.sum(v, axis=0), q + jnp.sum(v * v, axis=0)

        first, square = lax.fori_loop(0, frames * rows, add, (first, square))
        part = jnp.concatenate(
            [
                jnp.sum(first, axis=0, keepdims=True),
                jnp.sum(square, axis=0, keepdims=True),
                jnp.zeros((STAT_ROWS - 2, chans), jnp.float32),
            ],
            axis=0,
        )
        for axis, me, count, slots, send, recv in (
            ("rows", row, row_count, stat_a, sa_send, sa_recv),
            ("tm", tm, tm_count, stat_b, sb_send, sb_recv),
        ):
            slots[phase, 0] = part
            copies = []
            for k in range(1, count):
                copy = pltpu.make_async_remote_copy(
                    src_ref=slots.at[phase, 0], dst_ref=slots.at[phase, k],
                    send_sem=send.at[phase, k], recv_sem=recv.at[phase, k],
                    device_id={axis: lax.rem(me + k, count)},
                )
                copy.start()
                copies.append(copy)
            for copy in copies:
                copy.wait_recv()
            part = jnp.sum(slots[phase], axis=0)
            for copy in copies:
                copy.wait_send()
        mean = group_total(part, size) / total
        average = mean[0:1]
        spread = mean[1:2] - average * average
        return average, spread

    def coefficients(stats, gain_ref, shift_ref):
        average, spread = stats
        factor = lax.rsqrt(spread + EPS) * gain_ref[...] * 0.5
        return average, factor, shift_ref[...] * 0.5

    edge = lax.broadcasted_iota(jnp.int32, (width, chans), 0)

    def activate(cell, coef, frame, place):
        average, factor, offset = coef
        half = (cell.astype(jnp.float32) - average) * factor + offset
        value = half + half * jnp.tanh(half)
        left = jnp.where(edge == 0, 0.0, pltpu.roll(value, 1, 0))
        right = jnp.where(edge == width - 1, 0.0, pltpu.roll(value, width - 1, 0))
        base = place * span
        act[frame, :, pl.ds(base, chans)] = left.astype(jnp.bfloat16)
        act[frame, :, pl.ds(base + chans, chans)] = value.astype(jnp.bfloat16)
        act[frame, :, pl.ds(base + 2 * chans, chans)] = right.astype(jnp.bfloat16)

    def activate_own(src, coef):
        for r in range(rows):
            @pl.loop(0, frames)
            def _(f):
                activate(src[f, r], coef, f + LEAD, r + 1)

    def activate_side(buf, coef, place, first, count):
        @pl.loop(first, first + count)
        def _(f):
            activate(buf[f], coef, f, place)

    def halos(phase, c, coef):
        @pl.when(has_prev)
        def _():
            c["next"].wait_recv()
            for r in range(rows):
                @pl.loop(0, LEAD)
                def _(f):
                    activate(pre[phase, f, r], coef, f, r + 1)

        for cond, buf, place, late, early, corner in (
            (has_up, up.at[phase], 0, "down_late", "down_early", "corner_up"),
            (has_dn, dn.at[phase], rows + 1, "up_late", "up_early", "corner_dn"),
        ):
            @pl.when(cond)
            def _():
                activate_side(buf, coef, place, frames, LEAD)
                c[early].wait_recv()
                activate_side(buf, coef, place, LEAD, frames - LEAD)

                @pl.when(has_prev)
                def _():
                    c[corner].wait_recv()
                    activate_side(buf, coef, place, 0, LEAD)

        @pl.when(jnp.logical_not(has_prev))
        def _():
            for f in range(LEAD):
                act[f] = act[LEAD]

    def conv(frame, big, bias_ref):
        summed = jnp.dot(act[frame], big[0], preferred_element_type=jnp.float32)
        for i in range(1, 3):
            summed = summed + jnp.dot(act[frame + i], big[i], preferred_element_type=jnp.float32)
        return [summed[:, o * chans : (o + 1) * chans] + bias_ref[...] for o in range(rows)]

    ahead = halo(0, x_ref)
    send_late(ahead)
    send_early(ahead)

    for big in (big1, big2):
        for i in range(3):
            for o in range(rows):
                cols = pl.ds(o * chans, chans)
                if o > 0:
                    big[i, pl.ds(0, o * span), cols] = jnp.zeros((o * span, chans), jnp.bfloat16)
                rest = (rows - 1 - o) * span
                if rest > 0:
                    big[i, pl.ds(o * span + depth, rest), cols] = jnp.zeros((rest, chans), jnp.bfloat16)

    for cond, place in ((has_up, 0), (has_dn, rows + 1)):
        @pl.when(jnp.logical_not(cond))
        def _():
            for f in range(frames + LEAD):
                act[f, :, pl.ds(place * span, span)] = jnp.zeros((width, span), jnp.bfloat16)

    coef = coefficients(reduce_stats(0, x_ref), gain1_ref, shift1_ref)
    activate_own(x_ref, coef)
    forward(ahead)
    halos(0, ahead, coef)
    for copy in loads1:
        copy.wait()

    behind = halo(1, hid)

    def first_conv(f):
        for r, value in enumerate(conv(f, big1, bias1_ref)):
            hid[f, r] = value.astype(jnp.bfloat16)

    @pl.loop(frames - LEAD, frames)
    def _(f):
        first_conv(f)

    send_late(behind)

    @pl.loop(0, frames - LEAD)
    def _(f):
        first_conv(f)

    send_early(behind)
    coef = coefficients(reduce_stats(1, hid), gain2_ref, shift2_ref)
    activate_own(hid, coef)
    forward(behind)
    halos(1, behind, coef)
    for copy in loads2:
        copy.wait()

    @pl.loop(0, frames)
    def _(f):
        for r, value in enumerate(conv(f, big2, bias2_ref)):
            out_ref[f, r] = (value + x_ref[f, r].astype(jnp.float32)).astype(jnp.bfloat16)

    finish_sends(ahead)
    finish_sends(behind)


def body(tm_count, row_count, features, gain1, shift1, w1, bias1, gain2, shift2, w2, bias2):
    frames, rows, width, chans = features.shape
    lanes = (rows + 2) * 3 * chans
    vmem = pl.BlockSpec(memory_space=pltpu.VMEM)
    hbm = pl.BlockSpec(memory_space=pl.ANY)
    bf16, f32 = jnp.bfloat16, jnp.float32
    dma = pltpu.SemaphoreType.DMA
    return pl.pallas_call(
        functools.partial(kernel, tm_count, row_count),
        out_shape=jax.ShapeDtypeStruct(features.shape, bf16),
        in_specs=[vmem, vmem, vmem, hbm, vmem, vmem, vmem, hbm, vmem],
        out_specs=vmem,
        scratch_shapes=[
            pltpu.VMEM((frames + LEAD, width, lanes), bf16),
            pltpu.VMEM((3, lanes, rows * chans), bf16),
            pltpu.VMEM((3, lanes, rows * chans), bf16),
            pltpu.VMEM((frames, rows, width, chans), bf16),
            pltpu.VMEM((2, frames + LEAD, width, chans), bf16),
            pltpu.VMEM((2, frames + LEAD, width, chans), bf16),
            pltpu.VMEM((2, LEAD, rows, width, chans), bf16),
            pltpu.VMEM((STAT_ROWS, chans), f32),
            pltpu.VMEM((2, row_count, STAT_ROWS, chans), f32),
            pltpu.VMEM((2, tm_count, STAT_ROWS, chans), f32),
            dma((2, 3 * rows)),
            dma((2, 7)),
            dma((2, 7)),
            dma((2, row_count)),
            dma((2, row_count)),
            dma((2, tm_count)),
            dma((2, tm_count)),
        ],
        compiler_params=pltpu.CompilerParams(
            collective_id=0, has_side_effects=True, vmem_limit_bytes=40 * 1024 * 1024
        ),
        name="block",
    )(
        features, gain1.reshape(1, -1), shift1.reshape(1, -1), w1, bias1.reshape(1, -1),
        gain2.reshape(1, -1), shift2.reshape(1, -1), w2, bias2.reshape(1, -1),
    )


def solution(mesh):
    in_specs = (P("tm", "rows", None, None), P(), P(), P(), P(), P(), P(), P(), P())
    out_specs = P("tm", "rows", None, None)
    return jax.shard_map(
        functools.partial(body, mesh.shape["tm"], mesh.shape["rows"]),
        mesh=mesh, in_specs=in_specs, out_specs=out_specs, check_vma=False,
    )
```

time: 171 us -> 61.9 us (0.36)
  blocking collectives: 80.4 us -> 0 us
  Pallas kernels: 0 us -> 56.7 us
  waiting for transfers between devices: 42 us -> 0 us
  starting transfers between devices: 17.5 us -> 0 us
  matrix products: 13.6 us -> 0 us
  local copies, waits for them, and re-layouts: 11.6 us -> 4.96 us
  other arithmetic: 4.76 us -> 0 us
    psum x2 -> x0, blocking collectives: 80.4 us -> none  [moments(): lax.psum((group_sums(values), group_sums(values * values)), ('tm', 'rows'))]
    pallas_call x0 -> x1, Pallas kernels: none -> 56.7 us  [body(): pl.pallas_call(functools.partial(kernel, tm_count, row_count), out_shape=...]
    ppermute x6 -> x0, waiting for transfers between devices: 42 us -> none  [the longest x2 19.8 us: shifted(): return lax.ppermute(block, axis, route)]
    ppermute x6 -> x0, starting transfers between devices: 17.5 us -> none  [the longest x2 7.81 us: extended_2(): lax.ppermute(head, axis, [((i + 1) % count, i) for i in range(ends)])]
    dot_general x18 -> x0, matrix products: 13.6 us -> none  [valid_conv(): jnp.einsum('frwk,kc->frwc', columns, taps_block, preferred_element_type=j...]
    slice x8 -> x0, local copies, waits for them, and re-layouts: 9.93 us -> none  [the longest x6 9.84 us: valid_conv(): widened[time_tap:time_tap + out_frames, row_tap:row_tap + out_rows, col_t...]
    unnamed x14 -> x19, local copies, waits for them, and re-layouts: 0.42 us -> 4.96 us
    convert_element_type x2 -> x0, other arithmetic: 2.07 us -> none  [activate(): return jax.nn.silu(normed).astype(jnp.bfloat16)]
  transfers between devices with their start and end apart: 6 -> 0, of which waited for: 6 -> 0; matrix products, arithmetic and copies ran while one was open for 0% -> 0% of each run, Pallas kernels for 0% -> 0%
where the time goes in v1:
time: 61.9 us; the launch traced here: 61.7 us
  Pallas kernels  56.7 us (92%)
  local copies, waits for them, and re-layouts  4.96 us (8%)
    pallas_call x1, Pallas kernels, body(): pl.pallas_call(functools.partial(kernel, tm_count, row_count), out_shape=...  56.7 us
    unnamed x19, local copies, waits for them, and re-layouts  4.96 us

profile of v1, /device:TPU:12, one launch (start us, length us, event | category | flops | bytes accessed | tf_op | source)
XLA Modules:
  0.0 61.7 jit_solution(1314231617889219366)
XLA Ops:
  0.0 0.0 copy-start.6
  0.0 0.0 copy-start.7
  0.0 0.0 copy-start.8
  0.0 0.0 copy-start.3
  0.0 0.0 copy-start.4
  0.0 0.0 copy-start.5
  0.0 0.6 copy-done.6
  0.7 0.0 copy-done.7
  0.7 0.0 copy-done.8
  0.7 0.0 copy-done.3
  0.7 0.0 copy-done.4
  0.7 0.0 copy-done.5
  0.7 0.0 copy-start
  0.7 1.2 %copy-done = bf16[3456,128]{1,0:T(8,128)(2,1)S(1)} copy-done((bf16[3456,128]{1,0:T(8,128)(2,1)S(1)}, bf16[3456,128]{1,0:T(8,128)(2,1)}, u32[]{:S(2)}) %copy-start) | copy-done | bytes 884760
  1.9 0.0 copy-start.1
  1.9 1.2 %copy-done.1 = bf16[3456,128]{1,0:T(8,128)(2,1)S(1)} copy-done((bf16[3456,128]{1,0:T(8,128)(2,1)S(1)}, bf16[3456,128]{1,0:T(8,128)(2,1)}, u32[]{:S(2)}) %copy-start.1) | copy-done | bytes 884760
  3.1 0.0 copy-start.2
  3.1 1.1 %copy-done.2 = bf16[4,2,320,128]{3,2,1,0:T(8,128)(2,1)S(1)} copy-done((bf16[4,2,320,128]{3,2,1,0:T(8,128)(2,1)S(1)}, bf16[4,2,320,128]{3,2,1,0:T(8,128)(2,1)}, u32[]{:S(2)}) %copy-start.2) | copy-done | bytes 655384
  4.2 56.7 %block.1 = bf16[4,2,320,128]{3,2,1,0:T(8,128)(2,1)S(1)} custom-call(bf16[4,2,320,128]{3,2,1,0:T(8,128)(2,1)S(1)} %copy-done.2, f32[1,128]{1,0:T(1,128)S(1)} %bitcast.6, f32[1,128]{1,0:T(1,128)S(1)} %bitcast.7, bf16[3456,128]{1,0:T(8,128)(2,1)S(1)} %copy-done, f32[1,128]{1,0:T(1,128)S(1)} %bitcast.8, f32[1,128]{1,0:T(1,128)S(1)} %bitcast.9, ...), custom_call_target="tpu_custom_call" | custom-call | tf_op jit(solution)/shard_map/block/pallas_call | solution.py:305
  60.8 0.8 %copy.11 = bf16[4,2,320,128]{3,2,1,0:T(8,128)(2,1)} copy(bf16[4,2,320,128]{3,2,1,0:T(8,128)(2,1)S(1)} %block.1) | data formatting | bytes 1310720
Async XLA Ops:
  0.0 0.7 %copy-start.6 = (f32[128]{0:T(128)S(1)}, f32[128]{0:T(128)}, u32[]{:S(2)}) copy-start(f32[128]{0:T(128)} %param.14) | copy-start | bytes 1540
  0.0 0.7 %copy-start.7 = (f32[128]{0:T(128)S(1)}, f32[128]{0:T(128)}, u32[]{:S(2)}) copy-start(f32[128]{0:T(128)} %param.15) | copy-start | bytes 1540
  0.0 0.7 %copy-start.8 = (f32[128]{0:T(128)S(1)}, f32[128]{0:T(128)}, u32[]{:S(2)}) copy-start(f32[128]{0:T(128)} %param.17) | copy-start | bytes 1540
  0.0 0.7 %copy-start.3 = (f32[128]{0:T(128)S(1)}, f32[128]{0:T(128)}, u32[]{:S(2)}) copy-start(f32[128]{0:T(128)} %param.10) | copy-start | bytes 1540
  0.0 0.7 %copy-start.4 = (f32[128]{0:T(128)S(1)}, f32[128]{0:T(128)}, u32[]{:S(2)}) copy-start(f32[128]{0:T(128)} %param.11) | copy-start | bytes 1540
  0.0 0.7 %copy-start.5 = (f32[128]{0:T(128)S(1)}, f32[128]{0:T(128)}, u32[]{:S(2)}) copy-start(f32[128]{0:T(128)} %param.13) | copy-start | bytes 1540
  0.7 1.2 %copy-start = (bf16[3456,128]{1,0:T(8,128)(2,1)S(1)}, bf16[3456,128]{1,0:T(8,128)(2,1)}, u32[]{:S(2)}) copy-start(bf16[3456,128]{1,0:T(8,128)(2,1)} %w1_ref.1) | copy-start | bytes 2654212
  1.9 1.2 %copy-start.1 = (bf16[3456,128]{1,0:T(8,128)(2,1)S(1)}, bf16[3456,128]{1,0:T(8,128)(2,1)}, u32[]{:S(2)}) copy-start(bf16[3456,128]{1,0:T(8,128)(2,1)} %w2_ref.1) | copy-start | bytes 2654212
  3.1 1.1 %copy-start.2 = (bf16[4,2,320,128]{3,2,1,0:T(8,128)(2,1)S(1)}, bf16[4,2,320,128]{3,2,1,0:T(8,128)(2,1)}, u32[]{:S(2)}) copy-start(bf16[4,2,320,128]{3,2,1,0:T(8,128)(2,1)} %x_ref.1) | copy-start | bytes 1966084

commit v2 on v1

v2 whole, which is shorter than its diff:
```python
import functools

import jax
import jax.numpy as jnp
from jax import lax
from jax.experimental import pallas as pl
from jax.experimental.pallas import tpu as pltpu
from jax.sharding import PartitionSpec as P

GROUPS = 32
EPS = 1e-06
LEAD = 2
STAT_ROWS = 8


def group_total(values, size):
    lanes = values.shape[-1]
    lane = lax.broadcasted_iota(jnp.int32, values.shape, 1)
    step = 1
    while step < size:
        left = pltpu.roll(values, step, 1)
        right = pltpu.roll(values, lanes - step, 1)
        values = values + jnp.where((lane & step) == 0, right, left)
        step *= 2
    return values


def kernel(
    tm_count, row_count,
    x_hbm, gain1_hbm, shift1_hbm, w1_ref, bias1_hbm, gain2_hbm, shift2_hbm, w2_ref, bias2_hbm,
    out_hbm,
    x_ref, raw, hid, act, big1, big2, stage, out_buf, small, stat_a, stat_b,
    load_sem, w_sem, send_sem, recv_sem, sa_send, sa_recv, sb_send, sb_recv, store_sem,
):
    frames, rows, width, chans = x_ref.shape
    window = raw.shape[2]
    half = width // 2
    pad = window - half
    tall = 2 * rows
    early, late = frames - LEAD, LEAD
    tm = lax.axis_index("tm")
    row = lax.axis_index("rows")
    side = lax.rem(row, 2)
    pair = row // 2
    partner = {"rows": row + 1 - 2 * side}
    has_up = pair > 0
    has_dn = pair < row_count // 2 - 1
    has_prev = tm > 0
    has_next = tm < tm_count - 1
    left_side = side == 0
    above_row = jnp.maximum(row - 2, side)
    below_row = jnp.minimum(row + 2, row_count - 2 + side)
    above, below = {"rows": above_row}, {"rows": below_row}
    above_across = {"rows": above_row + 1 - 2 * side}
    below_across = {"rows": below_row + 1 - 2 * side}
    after = {"tm": jnp.minimum(tm + 1, tm_count - 1)}
    span = 3 * chans
    depth = 3 * span
    size = chans // GROUPS
    total = float(frames * rows * width * size * tm_count * row_count)

    def aligned(value):
        return pl.multiple_of(value, 16)

    mine = pl.ds(aligned(side * (half - pad)), window)
    theirs = pl.ds(aligned((1 - side) * (half - pad)), window)
    own_rows = pl.ds(1 + side * rows, rows)
    own_cols = pl.ds(aligned(side * pad), half)
    edge_src = pl.ds(aligned(half - pad - side * (half - 2 * pad)), pad)
    edge_dst = pl.ds(aligned(side * half), pad)
    half_cols = pl.ds(aligned(side * half), half)

    def weight_copies(which, src, dst):
        return [
            pltpu.make_async_copy(
                src.at[pl.ds(i * depth, depth)],
                dst.at[i, pl.ds(o * span, depth), pl.ds(o * chans, chans)],
                w_sem.at[which, i * rows + o],
            )
            for i in range(3)
            for o in range(rows)
        ]

    load_x = pltpu.make_async_copy(x_hbm, x_ref, load_sem.at[0])
    load_raw = pltpu.make_async_copy(
        x_hbm.at[:, :, mine], raw.at[pl.ds(LEAD, frames), own_rows], load_sem.at[1]
    )
    load_small = [
        pltpu.make_async_copy(src, small.at[n], load_sem.at[2 + n])
        for n, src in enumerate((gain1_hbm, shift1_hbm, bias1_hbm, gain2_hbm, shift2_hbm, bias2_hbm))
    ]
    loads1 = weight_copies(0, w1_ref, big1)
    loads2 = weight_copies(1, w2_ref, big2)
    for copy in [load_x, load_raw] + load_small + loads1 + loads2:
        copy.start()

    barrier = pltpu.get_barrier_semaphore()
    for k in range(1, row_count):
        pl.semaphore_signal(barrier, inc=1, device_id={"rows": lax.rem(row + k, row_count)})
    for k in range(1, tm_count):
        pl.semaphore_signal(barrier, inc=1, device_id={"tm": lax.rem(tm + k, tm_count)})

    used = [0]

    def remote(source, target, device):
        n = used[0]
        used[0] += 1
        return pltpu.make_async_remote_copy(
            src_ref=source, dst_ref=target, send_sem=send_sem.at[n], recv_sem=recv_sem.at[n],
            device_id=device,
        )

    parts = (pl.ds(LEAD + early, late), pl.ds(LEAD, early))
    source_parts = (pl.ds(early, late), pl.ds(0, early))

    swap = [
        remote(x_hbm.at[s, :, theirs], raw.at[d, own_rows], partner)
        for s, d in zip(source_parts, parts)
    ]

    def halo_copies(buf, cols):
        ups = [remote(buf.at[d, 1, cols], buf.at[d, tall + 1, cols], above) for d in parts]
        dns = [remote(buf.at[d, tall, cols], buf.at[d, 0, cols], below) for d in parts]
        first = pl.ds(0, LEAD)
        nexts = [
            remote(buf.at[parts[0], r], buf.at[first, r], after)
            for r in (pl.ds(1, tall), 0, tall + 1)
        ]
        return ups, dns, nexts

    ups1, dns1, nexts1 = halo_copies(raw, pl.ds(0, window))
    ups2, dns2, nexts2 = halo_copies(hid, own_cols)
    across = [
        remote(hid.at[d, pl.ds(1, tall), edge_src], hid.at[d, pl.ds(1, tall), edge_dst], partner)
        for d in parts
    ]
    ups_across = [
        remote(hid.at[d, 1, edge_src], hid.at[d, tall + 1, edge_dst], above_across) for d in parts
    ]
    dns_across = [
        remote(hid.at[d, tall, edge_src], hid.at[d, 0, edge_dst], below_across) for d in parts
    ]
    gives = [
        remote(stage.at[f], out_buf.at[f, :, half_cols], partner) for f in range(frames)
    ]

    def when(cond, fn):
        pl.when(cond)(fn)

    def local_stats(cells):
        def add(n, carry):
            s, q = carry
            v = cells(n).astype(jnp.float32)
            v = v.reshape(v.shape[0] // 8, 8, chans)
            return s + jnp.sum(v, axis=0), q + jnp.sum(v * v, axis=0)

        zero = jnp.zeros((8, chans), jnp.float32)
        return zero, add

    def summed_part(count, cells):
        zero, add = local_stats(cells)
        first, square = lax.fori_loop(0, count, add, (zero, zero))
        return jnp.concatenate(
            [
                jnp.sum(first, axis=0, keepdims=True),
                jnp.sum(square, axis=0, keepdims=True),
                jnp.zeros((STAT_ROWS - 2, chans), jnp.float32),
            ],
            axis=0,
        )

    def send_stats(phase, part, axis, me, count, slots, send, recv):
        slots[phase, 0] = part
        copies = []
        for k in range(1, count):
            copy = pltpu.make_async_remote_copy(
                src_ref=slots.at[phase, 0], dst_ref=slots.at[phase, k],
                send_sem=send.at[phase, k], recv_sem=recv.at[phase, k],
                device_id={axis: lax.rem(me + k, count)},
            )
            copy.start()
            copies.append(copy)
        return copies

    def stats_rows(phase, part):
        return send_stats(phase, part, "rows", row, row_count, stat_a, sa_send, sa_recv)

    def stats_tm(phase, part):
        return send_stats(phase, part, "tm", tm, tm_count, stat_b, sb_send, sb_recv)

    def collect(phase, copies, slots):
        for copy in copies:
            copy.wait_recv()
        return jnp.sum(slots[phase], axis=0)

    def coefficients(part, gain, shift):
        mean = group_total(part, size) / total
        average = mean[0:1]
        spread = mean[1:2] - average * average
        return average, lax.rsqrt(spread + EPS) * gain * 0.5, shift * 0.5

    edge = lax.broadcasted_iota(jnp.int32, (window, chans), 0)

    def activate(cell, coef, frame, place):
        average, factor, offset = coef
        h = (cell.astype(jnp.float32) - average) * factor + offset
        value = h + h * jnp.tanh(h)
        left = jnp.where(edge == 0, 0.0, pltpu.roll(value, 1, 0))
        right = jnp.where(edge == window - 1, 0.0, pltpu.roll(value, window - 1, 0))
        base = pl.multiple_of(place * span, chans)
        act[frame, :, pl.ds(base, chans)] = left.astype(jnp.bfloat16)
        act[frame, :, pl.ds(base + chans, chans)] = value.astype(jnp.bfloat16)
        act[frame, :, pl.ds(base + 2 * chans, chans)] = right.astype(jnp.bfloat16)

    def activate_block(buf, coef, first, count, top, height):
        @pl.loop(0, count * height)
        def _(n):
            f, r = first + n // height, top + n % height
            activate(buf[f, r], coef, f, r)

    def activate_edges(buf, coef, ups, dns, ups_more, dns_more, nexts, part):
        first, count = ((LEAD + early, late), (LEAD, early))[part]
        for cond, copies, more, place in (
            (has_up, dns, dns_more, 0), (has_dn, ups, ups_more, tall + 1)
        ):
            @pl.when(cond)
            def _():
                if part == 1:
                    copies[part].wait_recv()
                    if more:
                        more[part].wait_recv()
                activate_block(buf, coef, first, count, place, 1)

    def activate_lead(buf, coef, nexts):
        @pl.when(has_prev)
        def _():
            nexts[0].wait_recv()
            activate_block(buf, coef, 0, LEAD, 1, tall)
            for cond, copy, place in ((has_up, nexts[1], 0), (has_dn, nexts[2], tall + 1)):
                @pl.when(cond)
                def _():
                    copy.wait_recv()
                    activate_block(buf, coef, 0, LEAD, place, 1)

        @pl.when(jnp.logical_not(has_prev))
        def _():
            for f in range(LEAD):
                act[f] = act[LEAD]

    def forward_edges(ups, dns, ups_more, dns_more, nexts):
        for cond, copies, more, copy in (
            (has_up, dns, dns_more, nexts[1]), (has_dn, ups, ups_more, nexts[2])
        ):
            @pl.when(cond)
            def _():
                copies[0].wait_recv()
                if more:
                    more[0].wait_recv()
                when(has_next, copy.start)

    def conv(frame, group, big, bias):
        cells = lambda i: act[frame + i, own_cols, group * rows * span : (group * rows + rows + 2) * span]
        summed = jnp.dot(cells(0), big[0], preferred_element_type=jnp.float32)
        for i in range(1, 3):
            summed = summed + jnp.dot(cells(i), big[i], preferred_element_type=jnp.float32)
        return [summed[:, o * chans : (o + 1) * chans] + bias for o in range(rows)]

    load_x.wait()
    part = summed_part(frames * rows, lambda n: x_ref[n // rows, n % rows])
    pl.semaphore_wait(barrier, row_count + tm_count - 2)
    copies_a1 = stats_rows(0, part)
    for copy in swap:
        copy.start()
    load_raw.wait()
    for p in range(2):
        when(jnp.logical_and(left_side, has_up), ups1[p].start)
        when(jnp.logical_and(side == 1, has_dn), dns1[p].start)

    for big in (big1, big2):
        for i in range(3):
            for o in range(rows):
                cols = pl.ds(o * chans, chans)
                if o > 0:
                    big[i, pl.ds(0, o * span), cols] = jnp.zeros((o * span, chans), jnp.bfloat16)
                rest = (rows - 1 - o) * span
                if rest > 0:
                    big[i, pl.ds(o * span + depth, rest), cols] = jnp.zeros((rest, chans), jnp.bfloat16)

    for cond, place in ((has_up, 0), (has_dn, tall + 1)):
        @pl.when(jnp.logical_not(cond))
        def _():
            for f in range(frames + LEAD):
                act[f, :, pl.ds(place * span, span)] = jnp.zeros((window, span), jnp.bfloat16)

    for copy in load_small:
        copy.wait()
    copies_b1 = stats_tm(0, collect(0, copies_a1, stat_a))

    def forward_swapped(p):
        swap[p].wait_recv()
        when(jnp.logical_and(side == 1, has_up), ups1[p].start)
        when(jnp.logical_and(left_side, has_dn), dns1[p].start)

    forward_swapped(0)
    when(has_next, nexts1[0].start)
    coef = coefficients(collect(0, copies_b1, stat_b), small[0], small[1])
    for r in range(rows):
        activate_block(raw, coef, LEAD, frames, 1 + side * rows + r, 1)
    forward_swapped(1)
    forward_edges(ups1, dns1, [], [], nexts1)
    for r in range(rows):
        activate_block(raw, coef, LEAD, frames, 1 + (1 - side) * rows + r, 1)
    for p in range(2):
        activate_edges(raw, coef, ups1, dns1, [], [], nexts1, p)
    activate_lead(raw, coef, nexts1)
    for copy in loads1:
        copy.wait()

    def first_conv(f):
        for g in range(2):
            for r, value in enumerate(conv(f, g, big1, small[2])):
                hid[f + LEAD, 1 + g * rows + r, own_cols] = value.astype(jnp.bfloat16)

    for p, (first, count) in enumerate(((early, late), (0, early))):
        @pl.loop(first, first + count)
        def _(f):
            first_conv(f)

        across[p].start()
        for cond, copies in ((has_up, (ups2, ups_across)), (has_dn, (dns2, dns_across))):
            for c in copies:
                when(cond, c[p].start)

    part = summed_part(
        frames * tall, lambda n: hid[LEAD + n // tall, 1 + n % tall, own_cols]
    )
    copies_a2 = stats_rows(1, part)
    across[0].wait_recv()
    when(has_next, nexts2[0].start)
    forward_edges(ups2, dns2, ups_across, dns_across, nexts2)
    copies_b2 = stats_tm(1, collect(1, copies_a2, stat_a))
    coef = coefficients(collect(1, copies_b2, stat_b), small[3], small[4])
    across[1].wait_recv()
    activate_block(hid, coef, LEAD, frames, 1, tall)
    for p in range(2):
        activate_edges(hid, coef, ups2, dns2, ups_across, dns_across, nexts2, p)
    activate_lead(hid, coef, nexts2)
    for copy in loads2:
        copy.wait()

    for f in range(frames):
        for g in range(2):
            values = conv(f, g, big2, small[5])
            results = [
                (value + raw[f + LEAD, 1 + g * rows + r, own_cols].astype(jnp.float32)).astype(jnp.bfloat16)
                for r, value in enumerate(values)
            ]

            @pl.when(side == g)
            def _():
                for r, value in enumerate(results):
                    out_buf[f, r, half_cols] = value

            @pl.when(side != g)
            def _():
                for r, value in enumerate(results):
                    stage[f, r] = value

        gives[f].start()

    stores = [
        pltpu.make_async_copy(out_buf.at[f], out_hbm.at[f], store_sem.at[f]) for f in range(frames)
    ]
    for f in range(frames):
        gives[f].wait_recv()
        stores[f].start()

    for copy in copies_a1 + copies_b1 + copies_a2 + copies_b2 + swap + across + gives:
        copy.wait_send()
    for cond, copies in (
        (has_up, ups1 + ups2 + ups_across),
        (has_dn, dns1 + dns2 + dns_across),
        (has_next, [nexts1[0], nexts2[0]]),
        (jnp.logical_and(has_next, has_up), [nexts1[1], nexts2[1]]),
        (jnp.logical_and(has_next, has_dn), [nexts1[2], nexts2[2]]),
    ):
        @pl.when(cond)
        def _():
            for copy in copies:
                copy.wait_send()
    for copy in stores:
        copy.wait()


def body(tm_count, row_count, features, gain1, shift1, w1, bias1, gain2, shift2, w2, bias2):
    frames, rows, width, chans = features.shape
    window = width // 2 + 16
    tall = 2 * rows
    lanes = (tall + 2) * 3 * chans
    hbm = pl.BlockSpec(memory_space=pl.ANY)
    bf16, f32 = jnp.bfloat16, jnp.float32
    dma = pltpu.SemaphoreType.DMA
    remote = 2 + 7 + 7 + 6 + frames
    return pl.pallas_call(
        functools.partial(kernel, tm_count, row_count),
        out_shape=jax.ShapeDtypeStruct(features.shape, bf16),
        in_specs=[hbm] * 9,
        out_specs=hbm,
        scratch_shapes=[
            pltpu.VMEM((frames, rows, width, chans), bf16),
            pltpu.VMEM((frames + LEAD, tall + 2, window, chans), bf16),
            pltpu.VMEM((frames + LEAD, tall + 2, window, chans), bf16),
            pltpu.VMEM((frames + LEAD, window, lanes), bf16),
            pltpu.VMEM((3, (rows + 2) * 3 * chans, rows * chans), bf16),
            pltpu.VMEM((3, (rows + 2) * 3 * chans, rows * chans), bf16),
            pltpu.VMEM((frames, rows, width // 2, chans), bf16),
            pltpu.VMEM((frames, rows, width, chans), bf16),
            pltpu.VMEM((6, 1, chans), f32),
            pltpu.VMEM((2, row_count, STAT_ROWS, chans), f32),
            pltpu.VMEM((2, tm_count, STAT_ROWS, chans), f32),
            dma((8,)),
            dma((2, 3 * rows)),
            dma((remote,)),
            dma((remote,)),
            dma((2, row_count)),
            dma((2, row_count)),
            dma((2, tm_count)),
            dma((2, tm_count)),
            dma((frames,)),
        ],
        compiler_params=pltpu.CompilerParams(
            collective_id=0, has_side_effects=True, vmem_limit_bytes=40 * 1024 * 1024
        ),
        name="block",
    )(
        features, gain1.reshape(1, -1), shift1.reshape(1, -1), w1, bias1.reshape(1, -1),
        gain2.reshape(1, -1), shift2.reshape(1, -1), w2, bias2.reshape(1, -1),
    )


def solution(mesh):
    in_specs = (P("tm", "rows", None, None), P(), P(), P(), P(), P(), P(), P(), P())
    out_specs = P("tm", "rows", None, None)
    return jax.shard_map(
        functools.partial(body, mesh.shape["tm"], mesh.shape["rows"]),
        mesh=mesh, in_specs=in_specs, out_specs=out_specs, check_vma=False,
    )
```

time: 61.9 us -> 51.2 us (0.83)
  the two profiles are of different devices: /device:TPU:12 before, /device:TPU:0 now
where the time goes in v2:
time: 51.2 us; the launch traced here: 51 us
  Pallas kernels  46 us (90%)
  local copies, waits for them, and re-layouts  4.98 us (10%)
    pallas_call x1, Pallas kernels, body(): pl.pallas_call(functools.partial(kernel, tm_count, row_count), out_shape=...  46 us
    unnamed x19, local copies, waits for them, and re-layouts  4.98 us

profile of v2, /device:TPU:0, one launch (start us, length us, event | category | flops | bytes accessed | tf_op | source)
XLA Modules:
  0.0 51.0 jit_solution(2726818016889305519)
XLA Ops:
  0.0 0.0 copy-start.6
  0.0 0.0 copy-start.7
  0.0 0.0 copy-start.8
  0.0 0.0 copy-start.3
  0.0 0.0 copy-start.4
  0.0 0.0 copy-start.5
  0.0 0.6 %copy-done.6 = f32[128]{0:T(128)S(1)} copy-done((f32[128]{0:T(128)S(1)}, f32[128]{0:T(128)}, u32[]{:S(2)}) %copy-start.6) | copy-done | bytes 536
  0.7 0.0 copy-done.7
  0.7 0.0 copy-done.8
  0.7 0.0 copy-done.3
  0.7 0.0 copy-done.4
  0.7 0.0 copy-done.5
  0.7 0.0 copy-start
  0.7 1.2 %copy-done = bf16[3456,128]{1,0:T(8,128)(2,1)S(1)} copy-done((bf16[3456,128]{1,0:T(8,128)(2,1)S(1)}, bf16[3456,128]{1,0:T(8,128)(2,1)}, u32[]{:S(2)}) %copy-start) | copy-done | bytes 884760
  1.9 0.0 copy-start.1
  1.9 1.2 %copy-done.1 = bf16[3456,128]{1,0:T(8,128)(2,1)S(1)} copy-done((bf16[3456,128]{1,0:T(8,128)(2,1)S(1)}, bf16[3456,128]{1,0:T(8,128)(2,1)}, u32[]{:S(2)}) %copy-start.1) | copy-done | bytes 884760
  3.1 0.0 copy-start.2
  3.1 1.1 %copy-done.2 = bf16[4,2,320,128]{3,2,1,0:T(8,128)(2,1)S(1)} copy-done((bf16[4,2,320,128]{3,2,1,0:T(8,128)(2,1)S(1)}, bf16[4,2,320,128]{3,2,1,0:T(8,128)(2,1)}, u32[]{:S(2)}) %copy-start.2) | copy-done | bytes 655384
  4.2 46.0 %block.1 = bf16[4,2,320,128]{3,2,1,0:T(8,128)(2,1)S(1)} custom-call(bf16[4,2,320,128]{3,2,1,0:T(8,128)(2,1)S(1)} %copy-done.2, f32[1,128]{1,0:T(1,128)S(1)} %bitcast.6, f32[1,128]{1,0:T(1,128)S(1)} %bitcast.7, bf16[3456,128]{1,0:T(8,128)(2,1)S(1)} %copy-done, f32[1,128]{1,0:T(1,128)S(1)} %bitcast.8, f32[1,128]{1,0:T(1,128)S(1)} %bitcast.9, ...), custom_call_target="tpu_custom_call" | custom-call | tf_op jit(solution)/shard_map/block/pallas_call | solution.py:404
  50.2 0.8 %copy.11 = bf16[4,2,320,128]{3,2,1,0:T(8,128)(2,1)} copy(bf16[4,2,320,128]{3,2,1,0:T(8,128)(2,1)S(1)} %block.1) | data formatting | bytes 1310720
Async XLA Ops:
  0.0 0.7 %copy-start.6 = (f32[128]{0:T(128)S(1)}, f32[128]{0:T(128)}, u32[]{:S(2)}) copy-start(f32[128]{0:T(128)} %param.14) | copy-start | bytes 1540
  0.0 0.7 %copy-start.7 = (f32[128]{0:T(128)S(1)}, f32[128]{0:T(128)}, u32[]{:S(2)}) copy-start(f32[128]{0:T(128)} %param.15) | copy-start | bytes 1540
  0.0 0.7 %copy-start.8 = (f32[128]{0:T(128)S(1)}, f32[128]{0:T(128)}, u32[]{:S(2)}) copy-start(f32[128]{0:T(128)} %param.17) | copy-start | bytes 1540
  0.0 0.7 %copy-start.3 = (f32[128]{0:T(128)S(1)}, f32[128]{0:T(128)}, u32[]{:S(2)}) copy-start(f32[128]{0:T(128)} %param.10) | copy-start | bytes 1540
  0.0 0.7 %copy-start.4 = (f32[128]{0:T(128)S(1)}, f32[128]{0:T(128)}, u32[]{:S(2)}) copy-start(f32[128]{0:T(128)} %param.11) | copy-start | bytes 1540
  0.0 0.7 %copy-start.5 = (f32[128]{0:T(128)S(1)}, f32[128]{0:T(128)}, u32[]{:S(2)}) copy-start(f32[128]{0:T(128)} %param.13) | copy-start | bytes 1540
  0.7 1.2 %copy-start = (bf16[3456,128]{1,0:T(8,128)(2,1)S(1)}, bf16[3456,128]{1,0:T(8,128)(2,1)}, u32[]{:S(2)}) copy-start(bf16[3456,128]{1,0:T(8,128)(2,1)} %w1_ref.1) | copy-start | bytes 2654212
  1.9 1.2 %copy-start.1 = (bf16[3456,128]{1,0:T(8,128)(2,1)S(1)}, bf16[3456,128]{1,0:T(8,128)(2,1)}, u32[]{:S(2)}) copy-start(bf16[3456,128]{1,0:T(8,128)(2,1)} %w2_ref.1) | copy-start | bytes 2654212
  3.1 1.1 %copy-start.2 = (bf16[4,2,320,128]{3,2,1,0:T(8,128)(2,1)S(1)}, bf16[4,2,320,128]{3,2,1,0:T(8,128)(2,1)}, u32[]{:S(2)}) copy-start(bf16[4,2,320,128]{3,2,1,0:T(8,128)(2,1)} %x_hbm.1) | copy-start | bytes 1966084

commit v3 on v2

--- a/solution.py
+++ b/solution.py
@@ -258,12 +258,16 @@
                     more[0].wait_recv()
                 when(has_next, copy.start)
 
-    def conv(frame, group, big, bias):
-        cells = lambda i: act[frame + i, own_cols, group * rows * span : (group * rows + rows + 2) * span]
+    def conv(frame, count, group, big, bias):
+        lanes = slice(group * rows * span, (group * rows + rows + 2) * span)
+        cells = lambda i: act[pl.ds(frame + i, count), own_cols, lanes].reshape(count * half, -1)
         summed = jnp.dot(cells(0), big[0], preferred_element_type=jnp.float32)
         for i in range(1, 3):
             summed = summed + jnp.dot(cells(i), big[i], preferred_element_type=jnp.float32)
-        return [summed[:, o * chans : (o + 1) * chans] + bias for o in range(rows)]
+        return [
+            (summed[:, o * chans : (o + 1) * chans] + bias).reshape(count, half, chans)
+            for o in range(rows)
+        ]
 
     load_x.wait()
     part = summed_part(frames * rows, lambda n: x_ref[n // rows, n % rows])
@@ -316,15 +320,10 @@
     for copy in loads1:
         copy.wait()
 
-    def first_conv(f):
+    for p, (first, count) in enumerate(((early, late), (0, early))):
         for g in range(2):
-            for r, value in enumerate(conv(f, g, big1, small[2])):
-                hid[f + LEAD, 1 + g * rows + r, own_cols] = value.astype(jnp.bfloat16)
-
-    for p, (first, count) in enumerate(((early, late), (0, early))):
-        @pl.loop(first, first + count)
-        def _(f):
-            first_conv(f)
+            for r, value in enumerate(conv(first, count, g, big1, small[2])):
+                hid[parts[p], 1 + g * rows + r, own_cols] = value.astype(jnp.bfloat16)
 
         across[p].start()
         for cond, copies in ((has_up, (ups2, ups_across)), (has_dn, (dns2, dns_across))):
@@ -348,25 +347,27 @@
     for copy in loads2:
         copy.wait()
 
-    for f in range(frames):
+    for first, count in ((0, early), (early, late)):
+        block = pl.ds(first, count)
         for g in range(2):
-            values = conv(f, g, big2, small[5])
+            values = conv(first, count, g, big2, small[5])
             results = [
-                (value + raw[f + LEAD, 1 + g * rows + r, own_cols].astype(jnp.float32)).astype(jnp.bfloat16)
+                (value + raw[pl.ds(first + LEAD, count), 1 + g * rows + r, own_cols].astype(jnp.float32)).astype(jnp.bfloat16)
                 for r, value in enumerate(values)
             ]
 
             @pl.when(side == g)
             def _():
                 for r, value in enumerate(results):
-                    out_buf[f, r, half_cols] = value
+                    out_buf[block, r, half_cols] = value
 
             @pl.when(side != g)
             def _():
                 for r, value in enumerate(results):
-                    stage[f, r] = value
-
-        gives[f].start()
+                    stage[block, r] = value
+
+        for f in range(first, first + count):
+            gives[f].start()
 
     stores = [
         pltpu.make_async_copy(out_buf.at[f], out_hbm.at[f], store_sem.at[f]) for f in range(frames)
@@ -397,7 +398,7 @@
     window = width // 2 + 16
     tall = 2 * rows
     lanes = (tall + 2) * 3 * chans
-    hbm = pl.BlockSpec(memory_space=pl.ANY)
+    hbm = pl.BlockSpec(memory_space=pltpu.HBM)
     bf16, f32 = jnp.bfloat16, jnp.float32
     dma = pltpu.SemaphoreType.DMA
     remote = 2 + 7 + 7 + 6 + frames
@@ -429,7 +430,7 @@
             dma((frames,)),
         ],
         compiler_params=pltpu.CompilerParams(
-            collective_id=0, has_side_effects=True, vmem_limit_bytes=40 * 1024 * 1024
+            collective_id=0, has_side_effects=True, vmem_limit_bytes=65000 * 1024
         ),
         name="block",
     )(

time: 51.2 us -> 48.7 us (0.951)
  local copies, waits for them, and re-layouts: 4.98 us -> 1.97 us
  Pallas kernels: 46 us -> 46.6 us
    unnamed x19 -> x1, local copies, waits for them, and re-layouts: 4.98 us -> 1.97 us
    pallas_call x1, Pallas kernels: 46 us -> 46.6 us  [body(): pl.pallas_call(functools.partial(kernel, tm_count, row_count), out_shape=...]
where the time goes in v3:
time: 48.7 us; the launch traced here: 48.5 us
  Pallas kernels  46.6 us (96%)
  local copies, waits for them, and re-layouts  1.97 us (4%)
    pallas_call x1, Pallas kernels, body(): pl.pallas_call(functools.partial(kernel, tm_count, row_count), out_shape=...  46.6 us
    unnamed x1, local copies, waits for them, and re-layouts  1.97 us

profile of v3, /device:TPU:0, one launch (start us, length us, event | category | flops | bytes accessed | tf_op | source)
XLA Modules:
  0.0 48.5 jit_solution(16592891351636206663)
XLA Ops:
  0.0 46.6 %block.1 = bf16[4,2,320,128]{3,2,1,0:T(8,128)(2,1)} custom-call(bf16[4,2,320,128]{3,2,1,0:T(8,128)(2,1)} %x_hbm.1, f32[1,128]{1,0:T(1,128)} %bitcast.6, f32[1,128]{1,0:T(1,128)} %bitcast.7, bf16[3456,128]{1,0:T(8,128)(2,1)} %w1_ref.1, f32[1,128]{1,0:T(1,128)} %bitcast.8, f32[1,128]{1,0:T(1,128)} %bitcast.9, f32[1,128]{1,0:T(1,128)} %bitcast.10, ...), custom_call_target="tpu_custom_call" | custom-call | tf_op jit(solution)/shard_map/block/pallas_call | solution.py:405
  46.6 2.0 %copy.11 = bf16[4,2,320,128]{3,2,1,0:T(8,128)(2,1)} copy(bf16[4,2,320,128]{3,2,1,0:T(8,128)(2,1)} %block.1) | data formatting | bytes 1310720
